TPU v7x, 32 devices: a whole 2x2x4 slice. The times are simulated.
32 devices in a mesh: dom: 1, blk: 4 (over z), grp: 8 (over y, x, core), sub: 1.
Axes of the slice: x: 2, y: 2, z: 4, core: 2. Of those that a mesh axis runs over, the one named last changes fastest.
Arguments:
- records: bfloat16 [512, 8, 1024], P(('dom', 'blk', 'grp')), may hold values from -40 to 40
- flags: int32 [512, 8], P(('dom', 'blk', 'grp')), may hold values 0 or 1
Outputs:
- correlations: bfloat16 [256, 512, 3, 128], P('sub', ('dom', 'blk', 'grp'))
All inputs are finite; a program needn't handle non-finite values. No bound on the sum of `flags` on one device may be relied on, other than what follows from the above.
Results may differ from a plain program's by a relative error of at most 0.012.
Values may be sent and summed in bfloat16 or wider, within the bound.
A program may use at most 64 MiB of HBM per device.

v0:
```python
import functools

import jax
import jax.numpy as jnp
import ml_dtypes
import numpy as np
from jax import lax
from jax.experimental import pallas as pl
from jax.experimental.pallas import tpu as pltpu
from jax.sharding import PartitionSpec as P

LAGS = 256
STEPS = 3
LANES = 128
GROUP = 16
MESH = pl.DeviceIdType.MESH


def dft_tables(length):
    bins = length // 2
    phase = np.mod(np.arange(length)[:, None] * np.arange(bins)[None, :], length)
    angle = 2.0 * np.pi * phase / length
    return np.cos(angle).astype(np.float32), (-np.sin(angle)).astype(np.float32)


def lag_tables(length):
    bins = length // 2
    phase = np.mod((np.arange(LAGS) - LAGS // 2)[:, None] * np.arange(bins)[None, :], length)
    angle = 2.0 * np.pi * phase / length
    both = np.stack([np.cos(angle), -np.sin(angle)], axis=1).astype(np.float32)
    return both.astype(ml_dtypes.bfloat16)


def regroup_table(segs):
    per = LANES // GROUP
    table = np.zeros((segs, per, GROUP, per, segs, GROUP), np.float32)
    for s in range(segs):
        for q in range(per):
            for f in range(GROUP):
                table[s, q, f, q, s, f] = 1.0
    size = segs * LANES
    return table.reshape(size, size).astype(ml_dtypes.bfloat16)


def row_table(channels, segs):
    table = np.zeros((segs, channels, channels, segs), np.float32)
    for s in range(segs):
        for c in range(channels):
            table[s, c, c, s] = 1.0
    size = segs * channels
    return table.reshape(size, size).astype(ml_dtypes.bfloat16)


def mm(a, b):
    return jnp.dot(a, b, preferred_element_type=jnp.float32)


def mm_t(a, b):
    return lax.dot_general(a, b, (((1,), (1,)), ((), ())), preferred_element_type=jnp.float32)


def kernel(
    blks, grps, dims, normalise,
    rec_ref, flag_ref, row_ref, hi_hbm, lo_hbm, perm_hbm, lag_hbm,
    out_ref, count_ref,
    hi_ref, lo_ref, perm_ref, lag_ref, load_sem, buf, diag, cross, inv, wide, stage, recv_sem, hop_sem, peer_sem, sib_sem,
):
    channels, segs, bins, half = dims
    width = half * 2 * segs
    chunks = half // GROUP
    pair = channels // 2
    loads = [
        pltpu.make_async_copy(source, target, load_sem.at[n])
        for n, (source, target) in enumerate(
            ((hi_hbm, hi_ref), (lo_hbm, lo_ref), (perm_hbm, perm_ref), (lag_hbm, lag_ref)))
    ]
    for load in loads:
        load.start()
    b = lax.axis_index("blk")
    g = lax.axis_index("grp")
    sib = g + 1 - 2 * lax.rem(g, 2)
    peers = [lax.rem(g + 2 * d, grps) for d in range(1, grps // 2)]

    barrier = pltpu.get_barrier_semaphore()
    for k in range(1, STEPS):
        pl.semaphore_signal(barrier, inc=1, device_id={"blk": lax.rem(b + blks - k, blks)}, device_id_type=MESH)
    for other in peers + [sib]:
        pl.semaphore_signal(barrier, inc=1, device_id={"grp": other}, device_id_type=MESH)

    rec = mm(row_ref[...], rec_ref[...]).astype(jnp.bfloat16)
    loads[0].wait()
    spec = mm(rec, hi_ref[...])
    loads[1].wait()
    spec = spec + mm(rec, lo_ref[...])
    real = spec[:, :bins]
    imag = spec[:, bins:]
    power = real * real + imag * imag
    level = jnp.sum(power, axis=1, keepdims=True) / bins
    scale = 1.0 / jnp.sqrt(power[:, :half] + level + 1e-06)
    wide[...] = jnp.zeros_like(wide)
    wide[:, :segs] = flag_ref[...].astype(jnp.float32)
    flags = wide[...]
    pieces = [(real[:, :half] * scale).astype(jnp.bfloat16), (imag[:, :half] * scale).astype(jnp.bfloat16)]
    rows = []
    for t in range(half // LANES):
        for piece in pieces:
            rows.append(jnp.concatenate([
                piece[s * channels:(s + 1) * channels, t * LANES:(t + 1) * LANES]
                * flags[:, s:s + 1].astype(jnp.bfloat16)
                for s in range(segs)
            ], axis=1))
    loads[2].wait()
    regrouped = mm(jnp.concatenate(rows, axis=0), perm_ref[...]).astype(jnp.bfloat16)
    per = LANES // GROUP
    for t in range(half // LANES):
        for i in range(2):
            part = regrouped[(t * 2 + i) * channels:(t * 2 + i + 1) * channels]
            for q in range(per):
                at = ((t * per + q) * 2 + i) * LANES
                buf[0, g, :, at:at + LANES] = part[:, q * LANES:(q + 1) * LANES]
    buf[0, g, :, width:width + LANES] = flags.astype(jnp.bfloat16)

    pl.semaphore_wait(barrier, STEPS - 1 + len(peers) + 1)

    sent = []

    cut = width // 2
    spans = [(0, cut), (cut, width + LANES - cut)]
    steps = [(k, h) for k in range(STEPS) for h in range(2)]

    def piece(k, h, slot):
        return buf.at[k, slot, :, pl.ds(*spans[h])]

    def send(source, target, send_sem, landed, where):
        copy = pltpu.make_async_remote_copy(
            src_ref=source, dst_ref=target, send_sem=send_sem, recv_sem=landed,
            device_id=where, device_id_type=MESH,
        )
        copy.start()
        sent.append(copy)

    def arrived(k, h, slot):
        ref = piece(k, h, slot)
        pltpu.make_async_copy(ref, ref, recv_sem.at[k, h, slot]).wait()

    def hand(k, h, slot, n):
        ref = piece(k, h, slot)
        send(ref, ref, sib_sem.at[k, h, n], recv_sem.at[k, h, slot], {"grp": sib})

    def spread(k, h):
        ref = piece(k, h, g)
        for d, other in enumerate(peers):
            send(ref, ref, peer_sem.at[k, h, d], recv_sem.at[k, h, g], {"grp": other})
        hand(k, h, g, 0)

    def hopped(k):
        for h in range(2):
            arrived(k, h, g)
            spread(k, h)

    def forward(k, h):
        for d in range(len(peers)):
            slot = lax.rem(g + grps - 2 * (d + 1), grps)
            arrived(k, h, slot)
            hand(k, h, slot, d + 1)

    def gather(k, h):
        for d in range(grps // 2):
            arrived(k, h, lax.rem(sib + 2 * d, grps))

    spread(0, 0)
    for k in range(1, STEPS):
        for h in range(2):
            send(piece(0, h, g), piece(k, h, g), hop_sem.at[k, h], recv_sem.at[k, h, g],
                 {"blk": lax.rem(b + k, blks)})
    spread(0, 1)

    size = 2 * segs * GROUP
    same = (lax.broadcasted_iota(jnp.int32, (channels * GROUP, size), 0) % GROUP
            == lax.broadcasted_iota(jnp.int32, (channels * GROUP, size), 1) % GROUP)

    def build(q, carry):
        at = pl.multiple_of(q * size, size)
        first = buf[0, g, :, pl.ds(at, size)].astype(jnp.float32)
        second = jnp.concatenate([first[:, LANES:], -first[:, :LANES]], axis=1)
        for i, value in enumerate((first, second)):
            wide = jnp.broadcast_to(value[:, None, :], (channels, GROUP, size)).reshape(channels * GROUP, size)
            diag[q, i * channels * GROUP:(i + 1) * channels * GROUP, :] = jnp.where(same, wide, 0.0).astype(jnp.bfloat16)
        return carry

    lax.fori_loop(0, chunks // 2, build, 0)
    hopped(1)
    forward(0, 0)
    lax.fori_loop(chunks // 2, chunks, build, 0)
    hopped(2)
    forward(0, 1)
    loads[3].wait()
    block = grps * channels
    unroll = 4

    def multiply(group, carry, k):
        for u in range(unroll):
            q = group * unroll + u
            at = pl.multiple_of(q * size, size)
            other = buf[k, :, :, pl.ds(at, size)].reshape(block, size)
            product = mm_t(diag[q], other).astype(jnp.bfloat16).reshape(2, 2, pair, GROUP, block)
            low = pl.multiple_of(q * GROUP, GROUP)
            for i in range(2):
                for p in range(2):
                    cross[:, i, pl.ds(low, GROUP), p * block:(p + 1) * block] = product[i, p]
        return carry

    def lag(c, carry, k):
        total = mm(lag_ref[...], cross[c].reshape(2 * half, 2 * block)).astype(jnp.bfloat16)
        if normalise:
            total = (total.astype(jnp.float32) * inv[pl.ds(c, 1), :]).astype(jnp.bfloat16)
        total = total.astype(jnp.float32)
        stage[pl.ds(c, LAGS, stride=channels), :] = total[:, :block]
        stage[pl.ds(c + pair, LAGS, stride=channels), :] = total[:, block:]
        return carry

    def place(n, carry, k):
        low = pl.multiple_of(n * 16, 16)
        part = stage[pl.ds(pl.multiple_of(n * 16 * channels, 16), 16 * channels), :]
        out_ref[pl.ds(low, 16), k] = part.astype(jnp.bfloat16).reshape(16, channels, block)
        return carry

    groups = chunks // 2 // unroll
    for n, (k, h) in enumerate(steps):
        gather(k, h)
        lax.fori_loop(h * groups, (h + 1) * groups, functools.partial(multiply, k=k), 0)
        if n + 2 < len(steps):
            forward(*steps[n + 2])
        if h == 1:
            tile = buf[k, :, :, width:width + LANES].reshape(block, LANES)
            count = mm_t(flags.astype(jnp.bfloat16), tile)
            count_ref[:, k * block:(k + 1) * block] = count
            factor = lax.rsqrt(bins * jnp.maximum(count, 1.0))
            inv[:, :block] = factor[:pair]
            inv[:, block:] = factor[pair:]
            lax.fori_loop(0, pair, functools.partial(lag, k=k), 0)
            lax.fori_loop(0, LAGS // 16, functools.partial(place, k=k), 0)

    for copy in sent:
        copy.wait_send()


def on_device(records, flags):
    channels, segs, length = records.shape
    bins = length // 2
    splits = lax.axis_size("sub")
    blks = lax.axis_size("blk")
    grps = lax.axis_size("grp")
    half = bins // splits
    block = grps * channels
    cos, sin = dft_tables(length)
    lags = lag_tables(length)
    both = np.stack([cos, sin], axis=1)
    high = both.astype(ml_dtypes.bfloat16)
    low = (both - high.astype(np.float32)).astype(ml_dtypes.bfloat16)
    high, low, lags = jnp.asarray(high), jnp.asarray(low), jnp.asarray(lags)
    if splits > 1:
        first = lax.axis_index("sub") * half
        high = jnp.roll(high, -first, axis=2)
        low = jnp.roll(low, -first, axis=2)
        lags = lax.dynamic_slice_in_dim(lags, first, half, 2)
    width = half * 2 * segs + LANES
    vmem = pl.BlockSpec(memory_space=pltpu.VMEM)
    out, count = pl.pallas_call(
        functools.partial(kernel, blks, grps, (channels, segs, bins, half), splits == 1),
        out_shape=(
            jax.ShapeDtypeStruct((LAGS, STEPS, channels, block), jnp.bfloat16),
            jax.ShapeDtypeStruct((channels, STEPS * block), jnp.float32),
        ),
        in_specs=[vmem] * 3 + [pl.BlockSpec(memory_space=pltpu.HBM)] * 4,
        out_specs=(vmem, vmem),
        scratch_shapes=[
            pltpu.VMEM((length, 2 * bins), jnp.bfloat16),
            pltpu.VMEM((length, 2 * bins), jnp.bfloat16),
            pltpu.VMEM((segs * LANES, segs * LANES), jnp.bfloat16),
            pltpu.VMEM((LAGS, 2 * half), jnp.bfloat16),
            pltpu.SemaphoreType.DMA((4,)),
            pltpu.VMEM((STEPS, grps, channels, width), jnp.bfloat16),
            pltpu.VMEM((half // GROUP, 2 * channels * GROUP, 2 * segs * GROUP), jnp.bfloat16),
            pltpu.VMEM((channels // 2, 2, half, 2 * block), jnp.bfloat16),
            pltpu.VMEM((channels // 2, 2 * block), jnp.float32),
            pltpu.VMEM((channels, LANES), jnp.float32),
            pltpu.VMEM(((LAGS + 1) * channels, block), jnp.float32),
            pltpu.SemaphoreType.DMA((STEPS, 2, grps)),
            pltpu.SemaphoreType.DMA((STEPS, 2)),
            pltpu.SemaphoreType.DMA((STEPS, 2, max(grps // 2 - 1, 1))),
            pltpu.SemaphoreType.DMA((STEPS, 2, grps // 2)),
        ],
        compiler_params=pltpu.CompilerParams(
            collective_id=0, has_side_effects=True, vmem_limit_bytes=62 * 1024 * 1024
        ),
    )(
        records.reshape(channels * segs, length),
        flags,
        jnp.asarray(row_table(channels, segs)),
        high.reshape(length, 2 * bins),
        low.reshape(length, 2 * bins),
        jnp.asarray(regroup_table(segs)),
        lags.reshape(LAGS, 2 * half),
    )
    out = out.transpose(0, 2, 1, 3)
    if splits > 1:
        out = lax.psum_scatter(out, "sub", scatter_dimension=0, tiled=True).astype(jnp.float32)
        out = (out / jnp.sqrt(bins * jnp.maximum(count, 1.0)).reshape(1, channels, STEPS, block)).astype(jnp.bfloat16)
    return out


def solution(mesh):
    return jax.shard_map(
        on_device,
        mesh=mesh,
        in_specs=(P(("dom", "blk", "grp"), None, None), P(("dom", "blk", "grp"), None)),
        out_specs=P("sub", ("dom", "blk", "grp"), None, None),
        check_vma=False,
    )
```

profile of v0, /device:TPU:0, one launch (start us, length us, event | category | flops | bytes accessed | tf_op | source)
XLA Modules:
  0.0 60.7 jit_solution(8601985562424321351)
XLA Ops:
  0.0 1.4 %copy.8.flag_ref = s32[16,8]{1,0:T(8,128)} copy(s32[16,8]{0,1:T(8,128)} %param.8) | data formatting | bytes 1024 | tf_op args[1]
  1.4 55.2 %shard_map.73 = (bf16[256,3,16,128]{3,2,1,0:T(8,128)(2,1)}, f32[16,384]{1,0:T(8,128)}) custom-call(bf16[128,1024]{1,0:T(8,128)(2,1)} %bitcast.3, s32[16,8]{1,0:T(8,128)} %copy.8.flag_ref, bf16[128,128]{1,0:T(8,128)(2,1)} %constant.13.clone.row_ref, bf16[1024,1024]{1,0:T(8,128)(2,1)} %constant.17.hi_hbm, bf16[1024,1024]{1,0:T(8,128)(2,1)} %constant.18.lo_hbm, ...), custom_call_target="tpu_custom_call" | custom-call | tf_op jit(solution)/shard_map/pallas_call | solution.py:269
  56.6 4.1 %copy.10 = bf16[256,16,3,128]{3,1,2,0:T(8,128)(2,1)} copy(bf16[256,16,3,128]{3,1,2,0:T(8,128)(2,1)} %bitcast.2) | data formatting | bytes 6291456
where the time goes:
time: 60.9 us; the launch traced here: 60.7 us
  Pallas kernels  55.2 us (91%)
  local copies, waits for them, and re-layouts  5.45 us (9%)
    pallas_call x1, Pallas kernels, on_device(): pl.pallas_call(functools.partial(kernel, blks, grps, (channels, segs, bin...  55.2 us
    unnamed x2, local copies, waits for them, and re-layouts  5.45 us

commit v1 on v0

--- a/solution.py
+++ b/solution.py
@@ -13,6 +13,7 @@
 STEPS = 3
 LANES = 128
 GROUP = 16
+PIECES = 2
 MESH = pl.DeviceIdType.MESH
 
 
@@ -79,12 +80,18 @@
     b = lax.axis_index("blk")
     g = lax.axis_index("grp")
     sib = g + 1 - 2 * lax.rem(g, 2)
-    peers = [lax.rem(g + 2 * d, grps) for d in range(1, grps // 2)]
+    core = lax.rem(g, 2)
+    across = g + 2 - 4 * lax.rem(g // 2, 2)
+    along = g + 4 - 8 * lax.rem(g // 4, 2)
+    source = (1 - core) * across + core * along
+    target = core * across + (1 - core) * along
+    corner = across + along - g
+    held = (g, source, target, corner)
 
     barrier = pltpu.get_barrier_semaphore()
     for k in range(1, STEPS):
         pl.semaphore_signal(barrier, inc=1, device_id={"blk": lax.rem(b + blks - k, blks)}, device_id_type=MESH)
-    for other in peers + [sib]:
+    for other in (across, along, sib):
         pl.semaphore_signal(barrier, inc=1, device_id={"grp": other}, device_id_type=MESH)
 
     rec = mm(row_ref[...], rec_ref[...]).astype(jnp.bfloat16)
@@ -98,7 +105,9 @@
     level = jnp.sum(power, axis=1, keepdims=True) / bins
     scale = 1.0 / jnp.sqrt(power[:, :half] + level + 1e-06)
     wide[...] = jnp.zeros_like(wide)
-    wide[:, :segs] = flag_ref[...].astype(jnp.float32)
+    unit = (lax.broadcasted_iota(jnp.int32, (channels, channels), 0)
+            == lax.broadcasted_iota(jnp.int32, (channels, channels), 1)).astype(jnp.float32)
+    wide[:, :segs] = mm_t(unit, flag_ref[...].astype(jnp.float32))
     flags = wide[...]
     pieces = [(real[:, :half] * scale).astype(jnp.bfloat16), (imag[:, :half] * scale).astype(jnp.bfloat16)]
     rows = []
@@ -120,13 +129,13 @@
                 buf[0, g, :, at:at + LANES] = part[:, q * LANES:(q + 1) * LANES]
     buf[0, g, :, width:width + LANES] = flags.astype(jnp.bfloat16)
 
-    pl.semaphore_wait(barrier, STEPS - 1 + len(peers) + 1)
+    pl.semaphore_wait(barrier, STEPS - 1 + 3)
 
     sent = []
 
-    cut = width // 2
-    spans = [(0, cut), (cut, width + LANES - cut)]
-    steps = [(k, h) for k in range(STEPS) for h in range(2)]
+    cut = width // PIECES
+    spans = [(h * cut, cut if h < PIECES - 1 else width + LANES - h * cut) for h in range(PIECES)]
+    steps = [(k, h) for k in range(STEPS) for h in range(PIECES)]
 
     def piece(k, h, slot):
         return buf.at[k, slot, :, pl.ds(*spans[h])]
@@ -143,37 +152,47 @@
         ref = piece(k, h, slot)
         pltpu.make_async_copy(ref, ref, recv_sem.at[k, h, slot]).wait()
 
-    def hand(k, h, slot, n):
+    def give(k, h, slot, n, other, sem):
         ref = piece(k, h, slot)
-        send(ref, ref, sib_sem.at[k, h, n], recv_sem.at[k, h, slot], {"grp": sib})
-
-    def spread(k, h):
-        ref = piece(k, h, g)
-        for d, other in enumerate(peers):
-            send(ref, ref, peer_sem.at[k, h, d], recv_sem.at[k, h, g], {"grp": other})
-        hand(k, h, g, 0)
-
-    def hopped(k):
-        for h in range(2):
-            arrived(k, h, g)
-            spread(k, h)
-
-    def forward(k, h):
-        for d in range(len(peers)):
-            slot = lax.rem(g + grps - 2 * (d + 1), grps)
-            arrived(k, h, slot)
-            hand(k, h, slot, d + 1)
-
-    def gather(k, h):
-        for d in range(grps // 2):
-            arrived(k, h, lax.rem(sib + 2 * d, grps))
-
-    spread(0, 0)
-    for k in range(1, STEPS):
-        for h in range(2):
+        send(ref, ref, sem.at[k, h, n], recv_sem.at[k, h, slot], {"grp": other})
+
+    def spread(n):
+        if n < len(steps):
+            k, h = steps[n]
+            if k:
+                arrived(k, h, g)
+            give(k, h, g, 0, target, peer_sem)
+            give(k, h, g, 1, source, peer_sem)
+            give(k, h, g, 0, sib, sib_sem)
+
+    def forward(n):
+        if n < len(steps):
+            k, h = steps[n]
+            arrived(k, h, source)
+            give(k, h, source, 2, target, peer_sem)
+            give(k, h, source, 1, sib, sib_sem)
+            arrived(k, h, target)
+            give(k, h, target, 2, sib, sib_sem)
+
+    def finish(n):
+        if n < len(steps):
+            k, h = steps[n]
+            arrived(k, h, corner)
+            give(k, h, corner, 3, sib, sib_sem)
+
+    def gather(n):
+        k, h = steps[n]
+        for slot in held:
+            arrived(k, h, slot + 1 - 2 * lax.rem(slot, 2))
+
+    def hop(h):
+        for k in range(1, STEPS):
             send(piece(0, h, g), piece(k, h, g), hop_sem.at[k, h], recv_sem.at[k, h, g],
                  {"blk": lax.rem(b + k, blks)})
-    spread(0, 1)
+
+    for h in range(PIECES):
+        spread(h)
+        hop(h)
 
     size = 2 * segs * GROUP
     same = (lax.broadcasted_iota(jnp.int32, (channels * GROUP, size), 0) % GROUP
@@ -189,11 +208,12 @@
         return carry
 
     lax.fori_loop(0, chunks // 2, build, 0)
-    hopped(1)
-    forward(0, 0)
+    forward(0)
+    spread(PIECES)
     lax.fori_loop(chunks // 2, chunks, build, 0)
-    hopped(2)
-    forward(0, 1)
+    forward(1)
+    finish(0)
+    spread(PIECES + 1)
     loads[3].wait()
     block = grps * channels
     unroll = 4
@@ -225,13 +245,15 @@
         out_ref[pl.ds(low, 16), k] = part.astype(jnp.bfloat16).reshape(16, channels, block)
         return carry
 
-    groups = chunks // 2 // unroll
+    groups = chunks // PIECES // unroll
     for n, (k, h) in enumerate(steps):
-        gather(k, h)
+        forward(n + 2)
+        finish(n + 1)
+        if n + PIECES + 2 < len(steps):
+            spread(n + PIECES + 2)
+        gather(n)
         lax.fori_loop(h * groups, (h + 1) * groups, functools.partial(multiply, k=k), 0)
-        if n + 2 < len(steps):
-            forward(*steps[n + 2])
-        if h == 1:
+        if h == PIECES - 1:
             tile = buf[k, :, :, width:width + LANES].reshape(block, LANES)
             count = mm_t(flags.astype(jnp.bfloat16), tile)
             count_ref[:, k * block:(k + 1) * block] = count
@@ -269,7 +291,7 @@
     out, count = pl.pallas_call(
         functools.partial(kernel, blks, grps, (channels, segs, bins, half), splits == 1),
         out_shape=(
-            jax.ShapeDtypeStruct((LAGS, STEPS, channels, block), jnp.bfloat16),
+            pltpu.VMEM((LAGS, STEPS, channels, block), jnp.bfloat16),
             jax.ShapeDtypeStruct((channels, STEPS * block), jnp.float32),
         ),
         in_specs=[vmem] * 3 + [pl.BlockSpec(memory_space=pltpu.HBM)] * 4,
@@ -286,17 +308,17 @@
             pltpu.VMEM((channels // 2, 2 * block), jnp.float32),
             pltpu.VMEM((channels, LANES), jnp.float32),
             pltpu.VMEM(((LAGS + 1) * channels, block), jnp.float32),
-            pltpu.SemaphoreType.DMA((STEPS, 2, grps)),
-            pltpu.SemaphoreType.DMA((STEPS, 2)),
-            pltpu.SemaphoreType.DMA((STEPS, 2, max(grps // 2 - 1, 1))),
-            pltpu.SemaphoreType.DMA((STEPS, 2, grps // 2)),
+            pltpu.SemaphoreType.DMA((STEPS, PIECES, grps)),
+            pltpu.SemaphoreType.DMA((STEPS, PIECES)),
+            pltpu.SemaphoreType.DMA((STEPS, PIECES, 3)),
+            pltpu.SemaphoreType.DMA((STEPS, PIECES, grps // 2)),
         ],
         compiler_params=pltpu.CompilerParams(
-            collective_id=0, has_side_effects=True, vmem_limit_bytes=62 * 1024 * 1024
+            collective_id=0, has_side_effects=True, vmem_limit_bytes=52 * 1024 * 1024
         ),
     )(
         records.reshape(channels * segs, length),
-        flags,
+        flags.T,
         jnp.asarray(row_table(channels, segs)),
         high.reshape(length, 2 * bins),
         low.reshape(length, 2 * bins),

time: 60.9 us -> 51.7 us (0.85)
  Pallas kernels: 55.2 us -> 49.2 us
  local copies, waits for them, and re-layouts: 5.45 us -> 1.67 us
    pallas_call x1, Pallas kernels: 55.2 us -> 49.2 us  [on_device(): pl.pallas_call(functools.partial(kernel, blks, grps, (channels, segs, bin...]
    unnamed x2 -> x1, local copies, waits for them, and re-layouts: 5.45 us -> 1.67 us
where the time goes in v1:
time: 51.7 us; the launch traced here: 50.9 us
  Pallas kernels  49.2 us (95%)
  local copies, waits for them, and re-layouts  1.67 us (3%)
    pallas_call x1, Pallas kernels, on_device(): pl.pallas_call(functools.partial(kernel, blks, grps, (channels, segs, bin...  49.2 us
    unnamed x1, local copies, waits for them, and re-layouts  1.67 us

profile of v1, /device:TPU:0, one launch (start us, length us, event | category | flops | bytes accessed | tf_op | source)
XLA Modules:
  0.0 50.9 jit_solution(7674237231631830642)
XLA Ops:
  0.0 49.2 %shard_map.73 = (bf16[256,3,16,128]{3,2,1,0:T(8,128)(2,1)S(1)}, f32[16,384]{1,0:T(8,128)}) custom-call(bf16[128,1024]{1,0:T(8,128)(2,1)} %bitcast.4, s32[8,16]{1,0:T(8,128)} %bitcast.5, bf16[128,128]{1,0:T(8,128)(2,1)} %constant.13.clone.row_ref, bf16[1024,1024]{1,0:T(8,128)(2,1)} %constant.17.hi_hbm, bf16[1024,1024]{1,0:T(8,128)(2,1)} %constant.18.lo_hbm, ...), custom_call_target="tpu_custom_call" | custom-call | tf_op jit(solution)/shard_map/pallas_call | solution.py:291
  49.2 1.7 %copy.9 = bf16[256,16,3,128]{3,1,2,0:T(8,128)(2,1)} copy(bf16[256,16,3,128]{3,1,2,0:T(8,128)(2,1)S(1)} %bitcast.3) | data formatting | bytes 6291456

commit v2 on v1

--- a/solution.py
+++ b/solution.py
@@ -195,16 +195,17 @@
         hop(h)
 
     size = 2 * segs * GROUP
-    same = (lax.broadcasted_iota(jnp.int32, (channels * GROUP, size), 0) % GROUP
-            == lax.broadcasted_iota(jnp.int32, (channels * GROUP, size), 1) % GROUP)
+    few = GROUP // 2
+    same = (lax.broadcasted_iota(jnp.int32, (channels * few, size), 0) % few
+            == lax.broadcasted_iota(jnp.int32, (channels * few, size), 1) % few)
 
     def build(q, carry):
         at = pl.multiple_of(q * size, size)
         first = buf[0, g, :, pl.ds(at, size)].astype(jnp.float32)
         second = jnp.concatenate([first[:, LANES:], -first[:, :LANES]], axis=1)
         for i, value in enumerate((first, second)):
-            wide = jnp.broadcast_to(value[:, None, :], (channels, GROUP, size)).reshape(channels * GROUP, size)
-            diag[q, i * channels * GROUP:(i + 1) * channels * GROUP, :] = jnp.where(same, wide, 0.0).astype(jnp.bfloat16)
+            wide = jnp.broadcast_to(value[:, None, :], (channels, few, size)).reshape(channels * few, size)
+            diag[q, i * channels * few:(i + 1) * channels * few, :] = jnp.where(same, wide, 0.0).astype(jnp.bfloat16)
         return carry
 
     lax.fori_loop(0, chunks // 2, build, 0)
@@ -216,14 +217,18 @@
     spread(PIECES + 1)
     loads[3].wait()
     block = grps * channels
-    unroll = 4
+    unroll = min(16, chunks // PIECES)
+    upper = lax.broadcasted_iota(jnp.int32, (block, size), 1) % GROUP >= few
 
     def multiply(group, carry, k):
         for u in range(unroll):
             q = group * unroll + u
             at = pl.multiple_of(q * size, size)
             other = buf[k, :, :, pl.ds(at, size)].reshape(block, size)
-            product = mm_t(diag[q], other).astype(jnp.bfloat16).reshape(2, 2, pair, GROUP, block)
+            zero = jnp.zeros_like(other)
+            other = jnp.concatenate([jnp.where(upper, zero, other), jnp.where(upper, other, zero)], axis=0)
+            product = mm_t(diag[q], other).reshape(2, 2, pair, few, 2 * block)
+            product = jnp.concatenate([product[..., :block], product[..., block:]], axis=3).astype(jnp.bfloat16)
             low = pl.multiple_of(q * GROUP, GROUP)
             for i in range(2):
                 for p in range(2):
@@ -260,8 +265,8 @@
             factor = lax.rsqrt(bins * jnp.maximum(count, 1.0))
             inv[:, :block] = factor[:pair]
             inv[:, block:] = factor[pair:]
-            lax.fori_loop(0, pair, functools.partial(lag, k=k), 0)
-            lax.fori_loop(0, LAGS // 16, functools.partial(place, k=k), 0)
+            lax.fori_loop(0, pair, functools.partial(lag, k=k), 0, unroll=4)
+            lax.fori_loop(0, LAGS // 16, functools.partial(place, k=k), 0, unroll=4)
 
     for copy in sent:
         copy.wait_send()
@@ -303,7 +308,7 @@
             pltpu.VMEM((LAGS, 2 * half), jnp.bfloat16),
             pltpu.SemaphoreType.DMA((4,)),
             pltpu.VMEM((STEPS, grps, channels, width), jnp.bfloat16),
-            pltpu.VMEM((half // GROUP, 2 * channels * GROUP, 2 * segs * GROUP), jnp.bfloat16),
+            pltpu.VMEM((half // GROUP, channels * GROUP, 2 * segs * GROUP), jnp.bfloat16),
             pltpu.VMEM((channels // 2, 2, half, 2 * block), jnp.bfloat16),
             pltpu.VMEM((channels // 2, 2 * block), jnp.float32),
             pltpu.VMEM((channels, LANES), jnp.float32),

time: 51.7 us -> 45.3 us (0.88)
  Pallas kernels: 49.2 us -> 42.7 us
    pallas_call x1, Pallas kernels: 49.2 us -> 42.7 us  [on_device(): pl.pallas_call(functools.partial(kernel, blks, grps, (channels, segs, bin...]
where the time goes in v2:
time: 45.3 us; the launch traced here: 44.4 us
  Pallas kernels  42.7 us (94%)
  local copies, waits for them, and re-layouts  1.67 us (4%)
    pallas_call x1, Pallas kernels, on_device(): pl.pallas_call(functools.partial(kernel, blks, grps, (channels, segs, bin...  42.7 us
    unnamed x1, local copies, waits for them, and re-layouts  1.67 us

profile of v2, /device:TPU:0, one launch (start us, length us, event | category | flops | bytes accessed | tf_op | source)
XLA Modules:
  0.0 44.4 jit_solution(7271372327982012999)
XLA Ops:
  0.0 42.7 %shard_map.73 = (bf16[256,3,16,128]{3,2,1,0:T(8,128)(2,1)S(1)}, f32[16,384]{1,0:T(8,128)}) custom-call(bf16[128,1024]{1,0:T(8,128)(2,1)} %bitcast.4, s32[8,16]{1,0:T(8,128)} %bitcast.5, bf16[128,128]{1,0:T(8,128)(2,1)} %constant.13.clone.row_ref, bf16[1024,1024]{1,0:T(8,128)(2,1)} %constant.17.hi_hbm, bf16[1024,1024]{1,0:T(8,128)(2,1)} %constant.18.lo_hbm, ...), custom_call_target="tpu_custom_call" | custom-call | tf_op jit(solution)/shard_map/pallas_call | solution.py:296
  42.7 1.7 %copy.9 = bf16[256,16,3,128]{3,1,2,0:T(8,128)(2,1)} copy(bf16[256,16,3,128]{3,1,2,0:T(8,128)(2,1)S(1)} %bitcast.3) | data formatting | bytes 6291456

commit v3 on v2

--- a/solution.py
+++ b/solution.py
@@ -13,7 +13,12 @@
 STEPS = 3
 LANES = 128
 GROUP = 16
-PIECES = 2
+SPLIT = (0, 1, 2)
+PIECES = len(SPLIT) - 1
+CLIMB = ((1, 0), (1, 1), (2, 1))
+ORDER = (
+    ("s", 0), ("s", 1), ("f", 0), ("t", 0), ("b", 0), ("s", 2), ("f", 1), ("s", 3), ("c", 0), ("m", 0), ("s", 4), ("t", 1), ("f", 2), ("c", 1), ("t", 2), ("s", 5), ("b", 1), ("c", 2), ("m", 1), ("t", 3), ("f", 3), ("e", 0), ("c", 3), ("f", 4), ("m", 2), ("t", 4), ("t", 5), ("f", 5), ("m", 3), ("c", 4), ("e", 1), ("c", 5), ("m", 4), ("m", 5), ("e", 2),
+)
 MESH = pl.DeviceIdType.MESH
 
 
@@ -30,17 +35,6 @@
     angle = 2.0 * np.pi * phase / length
     both = np.stack([np.cos(angle), -np.sin(angle)], axis=1).astype(np.float32)
     return both.astype(ml_dtypes.bfloat16)
-
-
-def regroup_table(segs):
-    per = LANES // GROUP
-    table = np.zeros((segs, per, GROUP, per, segs, GROUP), np.float32)
-    for s in range(segs):
-        for q in range(per):
-            for f in range(GROUP):
-                table[s, q, f, q, s, f] = 1.0
-    size = segs * LANES
-    return table.reshape(size, size).astype(ml_dtypes.bfloat16)
 
 
 def row_table(channels, segs):
@@ -62,9 +56,9 @@
 
 def kernel(
     blks, grps, dims, normalise,
-    rec_ref, flag_ref, row_ref, hi_hbm, lo_hbm, perm_hbm, lag_hbm,
+    rec_ref, flag_ref, row_ref, hi_hbm, lag_hbm,
     out_ref, count_ref,
-    hi_ref, lo_ref, perm_ref, lag_ref, load_sem, buf, diag, cross, inv, wide, stage, recv_sem, hop_sem, peer_sem, sib_sem,
+    hi_ref, perm_ref, lag_ref, load_sem, buf, diag, cross, inv, wide, stage, recv_sem, hop_sem, peer_sem, sib_sem,
 ):
     channels, segs, bins, half = dims
     width = half * 2 * segs
@@ -73,9 +67,9 @@
     loads = [
         pltpu.make_async_copy(source, target, load_sem.at[n])
         for n, (source, target) in enumerate(
-            ((hi_hbm, hi_ref), (lo_hbm, lo_ref), (perm_hbm, perm_ref), (lag_hbm, lag_ref)))
+            ((hi_hbm, hi_ref), (lag_hbm, lag_ref)))
     ]
-    for load in loads:
+    for load in loads[:-1]:
         load.start()
     b = lax.axis_index("blk")
     g = lax.axis_index("grp")
@@ -89,16 +83,19 @@
     held = (g, source, target, corner)
 
     barrier = pltpu.get_barrier_semaphore()
-    for k in range(1, STEPS):
-        pl.semaphore_signal(barrier, inc=1, device_id={"blk": lax.rem(b + blks - k, blks)}, device_id_type=MESH)
+    pl.semaphore_signal(barrier, inc=1, device_id={"blk": lax.rem(b + blks - 1, blks)}, device_id_type=MESH)
     for other in (across, along, sib):
         pl.semaphore_signal(barrier, inc=1, device_id={"grp": other}, device_id_type=MESH)
 
+    per = LANES // GROUP
+    came = lax.broadcasted_iota(jnp.int32, (segs * LANES, 1), 0)
+    goes = came // GROUP % per * LANES + came // LANES * GROUP + came % GROUP
+    lane = lax.broadcasted_iota(jnp.int32, (segs * LANES, LANES), 1)
+    for q in range(per):
+        perm_ref[:, q * LANES:(q + 1) * LANES] = jnp.where(goes == lane + q * LANES, 1.0, 0.0).astype(jnp.bfloat16)
     rec = mm(row_ref[...], rec_ref[...]).astype(jnp.bfloat16)
     loads[0].wait()
     spec = mm(rec, hi_ref[...])
-    loads[1].wait()
-    spec = spec + mm(rec, lo_ref[...])
     real = spec[:, :bins]
     imag = spec[:, bins:]
     power = real * real + imag * imag
@@ -118,9 +115,7 @@
                 * flags[:, s:s + 1].astype(jnp.bfloat16)
                 for s in range(segs)
             ], axis=1))
-    loads[2].wait()
     regrouped = mm(jnp.concatenate(rows, axis=0), perm_ref[...]).astype(jnp.bfloat16)
-    per = LANES // GROUP
     for t in range(half // LANES):
         for i in range(2):
             part = regrouped[(t * 2 + i) * channels:(t * 2 + i + 1) * channels]
@@ -129,12 +124,14 @@
                 buf[0, g, :, at:at + LANES] = part[:, q * LANES:(q + 1) * LANES]
     buf[0, g, :, width:width + LANES] = flags.astype(jnp.bfloat16)
 
-    pl.semaphore_wait(barrier, STEPS - 1 + 3)
+    loads[-1].start()
+    pl.semaphore_wait(barrier, 4)
 
     sent = []
 
-    cut = width // PIECES
-    spans = [(h * cut, cut if h < PIECES - 1 else width + LANES - h * cut) for h in range(PIECES)]
+    bounds = [chunks * part // SPLIT[-1] for part in SPLIT]
+    edges = [2 * segs * GROUP * bound for bound in bounds[:-1]] + [width + LANES]
+    spans = [(low, high - low) for low, high in zip(edges[:-1], edges[1:])]
     steps = [(k, h) for k in range(STEPS) for h in range(PIECES)]
 
     def piece(k, h, slot):
@@ -156,43 +153,43 @@
         ref = piece(k, h, slot)
         send(ref, ref, sem.at[k, h, n], recv_sem.at[k, h, slot], {"grp": other})
 
+    def rise(k, h, slot, n):
+        send(piece(k, h, slot), piece(k + 1, h, slot), hop_sem.at[k, h, n], recv_sem.at[k + 1, h, slot],
+             {"blk": lax.rem(b + 1, blks)})
+
     def spread(n):
-        if n < len(steps):
-            k, h = steps[n]
-            if k:
-                arrived(k, h, g)
-            give(k, h, g, 0, target, peer_sem)
-            give(k, h, g, 1, source, peer_sem)
-            give(k, h, g, 0, sib, sib_sem)
+        k, h = steps[n]
+        if k:
+            arrived(k, h, g)
+        if k + 1 < STEPS:
+            rise(k, h, g, 0)
+        give(k, h, g, 0, target, peer_sem)
+        give(k, h, g, 1, source, peer_sem)
+        give(k, h, g, 0, sib, sib_sem)
 
     def forward(n):
-        if n < len(steps):
-            k, h = steps[n]
-            arrived(k, h, source)
+        k, h = steps[n]
+        arrived(k, h, source)
+        if (k, h) not in CLIMB:
             give(k, h, source, 2, target, peer_sem)
-            give(k, h, source, 1, sib, sib_sem)
-            arrived(k, h, target)
-            give(k, h, target, 2, sib, sib_sem)
+        give(k, h, source, 1, sib, sib_sem)
+
+    def relay(n):
+        k, h = steps[n]
+        arrived(k, h, target)
+        give(k, h, target, 2, sib, sib_sem)
 
     def finish(n):
-        if n < len(steps):
-            k, h = steps[n]
-            arrived(k, h, corner)
-            give(k, h, corner, 3, sib, sib_sem)
+        k, h = steps[n]
+        arrived(k, h, corner)
+        if (k + 1, h) in CLIMB:
+            rise(k, h, corner, 1)
+        give(k, h, corner, 3, sib, sib_sem)
 
     def gather(n):
         k, h = steps[n]
         for slot in held:
             arrived(k, h, slot + 1 - 2 * lax.rem(slot, 2))
-
-    def hop(h):
-        for k in range(1, STEPS):
-            send(piece(0, h, g), piece(k, h, g), hop_sem.at[k, h], recv_sem.at[k, h, g],
-                 {"blk": lax.rem(b + k, blks)})
-
-    for h in range(PIECES):
-        spread(h)
-        hop(h)
 
     size = 2 * segs * GROUP
     few = GROUP // 2
@@ -208,32 +205,18 @@
             diag[q, i * channels * few:(i + 1) * channels * few, :] = jnp.where(same, wide, 0.0).astype(jnp.bfloat16)
         return carry
 
-    lax.fori_loop(0, chunks // 2, build, 0)
-    forward(0)
-    spread(PIECES)
-    lax.fori_loop(chunks // 2, chunks, build, 0)
-    forward(1)
-    finish(0)
-    spread(PIECES + 1)
-    loads[3].wait()
     block = grps * channels
-    unroll = min(16, chunks // PIECES)
     upper = lax.broadcasted_iota(jnp.int32, (block, size), 1) % GROUP >= few
 
-    def multiply(group, carry, k):
-        for u in range(unroll):
-            q = group * unroll + u
-            at = pl.multiple_of(q * size, size)
-            other = buf[k, :, :, pl.ds(at, size)].reshape(block, size)
-            zero = jnp.zeros_like(other)
-            other = jnp.concatenate([jnp.where(upper, zero, other), jnp.where(upper, other, zero)], axis=0)
-            product = mm_t(diag[q], other).reshape(2, 2, pair, few, 2 * block)
-            product = jnp.concatenate([product[..., :block], product[..., block:]], axis=3).astype(jnp.bfloat16)
-            low = pl.multiple_of(q * GROUP, GROUP)
-            for i in range(2):
-                for p in range(2):
-                    cross[:, i, pl.ds(low, GROUP), p * block:(p + 1) * block] = product[i, p]
-        return carry
+    def multiply(q, k):
+        other = buf[k, :, :, q * size:(q + 1) * size].reshape(block, size)
+        zero = jnp.zeros_like(other)
+        other = jnp.concatenate([jnp.where(upper, zero, other), jnp.where(upper, other, zero)], axis=0)
+        product = mm_t(diag[q], other).reshape(2, 2, pair, few, 2 * block)
+        product = jnp.concatenate([product[..., :block], product[..., block:]], axis=3).astype(jnp.bfloat16)
+        for i in range(2):
+            for p in range(2):
+                cross[:, i, q * GROUP:(q + 1) * GROUP, p * block:(p + 1) * block] = product[i, p]
 
     def lag(c, carry, k):
         total = mm(lag_ref[...], cross[c].reshape(2 * half, 2 * block)).astype(jnp.bfloat16)
@@ -250,23 +233,30 @@
         out_ref[pl.ds(low, 16), k] = part.astype(jnp.bfloat16).reshape(16, channels, block)
         return carry
 
-    groups = chunks // PIECES // unroll
-    for n, (k, h) in enumerate(steps):
-        forward(n + 2)
-        finish(n + 1)
-        if n + PIECES + 2 < len(steps):
-            spread(n + PIECES + 2)
+    def prepare(n):
+        lax.fori_loop(bounds[n], bounds[n + 1], build, 0, unroll=2)
+
+    def combine(n):
+        k, h = steps[n]
         gather(n)
-        lax.fori_loop(h * groups, (h + 1) * groups, functools.partial(multiply, k=k), 0)
-        if h == PIECES - 1:
-            tile = buf[k, :, :, width:width + LANES].reshape(block, LANES)
-            count = mm_t(flags.astype(jnp.bfloat16), tile)
-            count_ref[:, k * block:(k + 1) * block] = count
-            factor = lax.rsqrt(bins * jnp.maximum(count, 1.0))
-            inv[:, :block] = factor[:pair]
-            inv[:, block:] = factor[pair:]
-            lax.fori_loop(0, pair, functools.partial(lag, k=k), 0, unroll=4)
-            lax.fori_loop(0, LAGS // 16, functools.partial(place, k=k), 0, unroll=4)
+        for q in range(bounds[h], bounds[h + 1]):
+            multiply(q, k)
+
+    def emit(k):
+        if k == 0:
+            loads[-1].wait()
+        tile = buf[k, :, :, width:width + LANES].reshape(block, LANES)
+        count = mm_t(flags.astype(jnp.bfloat16), tile)
+        count_ref[:, k * block:(k + 1) * block] = count
+        factor = lax.rsqrt(bins * jnp.maximum(count, 1.0))
+        inv[:, :block] = factor[:pair]
+        inv[:, block:] = factor[pair:]
+        lax.fori_loop(0, pair, functools.partial(lag, k=k), 0, unroll=4)
+        lax.fori_loop(0, LAGS // 16, functools.partial(place, k=k), 0, unroll=4)
+
+    acts = {"s": spread, "f": forward, "t": relay, "c": finish, "b": prepare, "m": combine, "e": emit}
+    for act, n in ORDER:
+        acts[act](n)
 
     for copy in sent:
         copy.wait_send()
@@ -284,12 +274,10 @@
     lags = lag_tables(length)
     both = np.stack([cos, sin], axis=1)
     high = both.astype(ml_dtypes.bfloat16)
-    low = (both - high.astype(np.float32)).astype(ml_dtypes.bfloat16)
-    high, low, lags = jnp.asarray(high), jnp.asarray(low), jnp.asarray(lags)
+    high, lags = jnp.asarray(high), jnp.asarray(lags)
     if splits > 1:
         first = lax.axis_index("sub") * half
         high = jnp.roll(high, -first, axis=2)
-        low = jnp.roll(low, -first, axis=2)
         lags = lax.dynamic_slice_in_dim(lags, first, half, 2)
     width = half * 2 * segs + LANES
     vmem = pl.BlockSpec(memory_space=pltpu.VMEM)
@@ -299,14 +287,13 @@
             pltpu.VMEM((LAGS, STEPS, channels, block), jnp.bfloat16),
             jax.ShapeDtypeStruct((channels, STEPS * block), jnp.float32),
         ),
-        in_specs=[vmem] * 3 + [pl.BlockSpec(memory_space=pltpu.HBM)] * 4,
+        in_specs=[vmem] * 3 + [pl.BlockSpec(memory_space=pltpu.HBM)] * 2,
         out_specs=(vmem, vmem),
         scratch_shapes=[
             pltpu.VMEM((length, 2 * bins), jnp.bfloat16),
-            pltpu.VMEM((length, 2 * bins), jnp.bfloat16),
             pltpu.VMEM((segs * LANES, segs * LANES), jnp.bfloat16),
             pltpu.VMEM((LAGS, 2 * half), jnp.bfloat16),
-            pltpu.SemaphoreType.DMA((4,)),
+            pltpu.SemaphoreType.DMA((2,)),
             pltpu.VMEM((STEPS, grps, channels, width), jnp.bfloat16),
             pltpu.VMEM((half // GROUP, channels * GROUP, 2 * segs * GROUP), jnp.bfloat16),
             pltpu.VMEM((channels // 2, 2, half, 2 * block), jnp.bfloat16),
@@ -314,7 +301,7 @@
             pltpu.VMEM((channels, LANES), jnp.float32),
             pltpu.VMEM(((LAGS + 1) * channels, block), jnp.float32),
             pltpu.SemaphoreType.DMA((STEPS, PIECES, grps)),
-            pltpu.SemaphoreType.DMA((STEPS, PIECES)),
+            pltpu.SemaphoreType.DMA((STEPS - 1, PIECES, 2)),
             pltpu.SemaphoreType.DMA((STEPS, PIECES, 3)),
             pltpu.SemaphoreType.DMA((STEPS, PIECES, grps // 2)),
         ],
@@ -326,8 +313,6 @@
         flags.T,
         jnp.asarray(row_table(channels, segs)),
         high.reshape(length, 2 * bins),
-        low.reshape(length, 2 * bins),
-        jnp.asarray(regroup_table(segs)),
         lags.reshape(LAGS, 2 * half),
     )
     out = out.transpose(0, 2, 1, 3)

time: 45.3 us -> 40.2 us (0.89); the launches traced: 44.4 us -> 39.9 us
  Pallas kernels: 42.7 us -> 38.2 us
    pallas_call x1, Pallas kernels: 42.7 us -> 38.2 us  [on_device(): pl.pallas_call(functools.partial(kernel, blks, grps, (channels, segs, bin...]
where the time goes in v3:
time: 40.2 us; the launch traced here: 39.9 us
  Pallas kernels  38.2 us (95%)
  local copies, waits for them, and re-layouts  1.67 us (4%)
    pallas_call x1, Pallas kernels, on_device(): pl.pallas_call(functools.partial(kernel, blks, grps, (channels, segs, bin...  38.2 us
    unnamed x1, local copies, waits for them, and re-layouts  1.67 us

profile of v3, /device:TPU:0, one launch (start us, length us, event | category | flops | bytes accessed | tf_op | source)
XLA Modules:
  0.0 39.9 jit_solution(17373338253751320783)
XLA Ops:
  0.0 38.2 %shard_map.55 = (bf16[256,3,16,128]{3,2,1,0:T(8,128)(2,1)S(1)}, f32[16,384]{1,0:T(8,128)}) custom-call(bf16[128,1024]{1,0:T(8,128)(2,1)} %bitcast.4, s32[8,16]{1,0:T(8,128)} %bitcast.5, bf16[128,128]{1,0:T(8,128)(2,1)} %constant.8.clone.row_ref, bf16[1024,1024]{1,0:T(8,128)(2,1)} %constant.11.hi_hbm, bf16[256,1024]{1,0:T(8,128)(2,1)} %constant.12.lag_hbm), custom_call_target="tpu_custom_call" | custom-call | tf_op jit(solution)/shard_map/pallas_call | solution.py:284
  38.2 1.7 %copy.7 = bf16[256,16,3,128]{3,1,2,0:T(8,128)(2,1)} copy(bf16[256,16,3,128]{3,1,2,0:T(8,128)(2,1)S(1)} %bitcast.3) | data formatting | bytes 6291456

commit v4 on v3

--- a/solution.py
+++ b/solution.py
@@ -17,7 +17,7 @@
 PIECES = len(SPLIT) - 1
 CLIMB = ((1, 0), (1, 1), (2, 1))
 ORDER = (
-    ("s", 0), ("s", 1), ("f", 0), ("t", 0), ("b", 0), ("s", 2), ("f", 1), ("s", 3), ("c", 0), ("m", 0), ("s", 4), ("t", 1), ("f", 2), ("c", 1), ("t", 2), ("s", 5), ("b", 1), ("c", 2), ("m", 1), ("t", 3), ("f", 3), ("e", 0), ("c", 3), ("f", 4), ("m", 2), ("t", 4), ("t", 5), ("f", 5), ("m", 3), ("c", 4), ("e", 1), ("c", 5), ("m", 4), ("m", 5), ("e", 2),
+    ("s", 0), ("s", 1), ("f", 0), ("t", 0), ("b", 0), ("s", 2), ("f", 1), ("s", 3), ("c", 0), ("m", 0), ("s", 4), ("t", 1), ("f", 2), ("c", 1), ("t", 2), ("s", 5), ("b", 1), ("c", 2), ("m", 1), ("t", 3), ("f", 3), ("e", 0), ("e", 1), ("p", 0), ("c", 3), ("f", 4), ("m", 2), ("t", 4), ("t", 5), ("f", 5), ("m", 3), ("c", 4), ("e", 2), ("e", 3), ("p", 1), ("c", 5), ("m", 4), ("g", 0), ("g", 1), ("m", 5), ("e", 4), ("p", 2),
 )
 MESH = pl.DeviceIdType.MESH
 
@@ -58,7 +58,7 @@
     blks, grps, dims, normalise,
     rec_ref, flag_ref, row_ref, hi_hbm, lag_hbm,
     out_ref, count_ref,
-    hi_ref, perm_ref, lag_ref, load_sem, buf, diag, cross, inv, wide, stage, recv_sem, hop_sem, peer_sem, sib_sem,
+    hi_ref, perm_ref, lag_ref, load_sem, buf, diag, cross, inv, wide, stage, acc, recv_sem, hop_sem, peer_sem, sib_sem,
 ):
     channels, segs, bins, half = dims
     width = half * 2 * segs
@@ -218,20 +218,30 @@
             for p in range(2):
                 cross[:, i, q * GROUP:(q + 1) * GROUP, p * block:(p + 1) * block] = product[i, p]
 
-    def lag(c, carry, k):
-        total = mm(lag_ref[...], cross[c].reshape(2 * half, 2 * block)).astype(jnp.bfloat16)
+    begun = bounds[-2] * GROUP // LANES * LANES
+
+    def table(low, high):
+        return jnp.concatenate([lag_ref[:, i * half + low:i * half + high] for i in range(2)], axis=1)
+
+    def early(j):
+        if begun:
+            for c in range(j * pair // 2, (j + 1) * pair // 2):
+                acc[c] = mm(table(0, begun), cross[c, :, :begun].reshape(2 * begun, 2 * block))
+
+    def lag(c, k):
+        if begun and k == STEPS - 1:
+            total = acc[c] + mm(table(begun, half), cross[c, :, begun:].reshape(2 * (half - begun), 2 * block))
+        else:
+            total = mm(lag_ref[...], cross[c].reshape(2 * half, 2 * block))
         if normalise:
-            total = (total.astype(jnp.float32) * inv[pl.ds(c, 1), :]).astype(jnp.bfloat16)
-        total = total.astype(jnp.float32)
+            total = total * inv[c:c + 1, :]
         stage[pl.ds(c, LAGS, stride=channels), :] = total[:, :block]
         stage[pl.ds(c + pair, LAGS, stride=channels), :] = total[:, block:]
-        return carry
-
-    def place(n, carry, k):
-        low = pl.multiple_of(n * 16, 16)
-        part = stage[pl.ds(pl.multiple_of(n * 16 * channels, 16), 16 * channels), :]
-        out_ref[pl.ds(low, 16), k] = part.astype(jnp.bfloat16).reshape(16, channels, block)
-        return carry
+
+    def place(k):
+        for n in range(LAGS // 16):
+            part = stage[n * 16 * channels:(n + 1) * 16 * channels, :]
+            out_ref[n * 16:(n + 1) * 16, k] = part.astype(jnp.bfloat16).reshape(16, channels, block)
 
     def prepare(n):
         lax.fori_loop(bounds[n], bounds[n + 1], build, 0, unroll=2)
@@ -242,19 +252,25 @@
         for q in range(bounds[h], bounds[h + 1]):
             multiply(q, k)
 
-    def emit(k):
-        if k == 0:
+    def emit(n):
+        k = n // 2
+        if n == 0:
             loads[-1].wait()
-        tile = buf[k, :, :, width:width + LANES].reshape(block, LANES)
-        count = mm_t(flags.astype(jnp.bfloat16), tile)
-        count_ref[:, k * block:(k + 1) * block] = count
-        factor = lax.rsqrt(bins * jnp.maximum(count, 1.0))
-        inv[:, :block] = factor[:pair]
-        inv[:, block:] = factor[pair:]
-        lax.fori_loop(0, pair, functools.partial(lag, k=k), 0, unroll=4)
-        lax.fori_loop(0, LAGS // 16, functools.partial(place, k=k), 0, unroll=4)
-
-    acts = {"s": spread, "f": forward, "t": relay, "c": finish, "b": prepare, "m": combine, "e": emit}
+        if n % 2 == 0:
+            tile = buf[k, :, :, width:width + LANES].reshape(block, LANES)
+            count = mm_t(flags.astype(jnp.bfloat16), tile)
+            count_ref[:, k * block:(k + 1) * block] = count
+            factor = lax.rsqrt(bins * jnp.maximum(count, 1.0))
+            inv[:, :block] = factor[:pair]
+            inv[:, block:] = factor[pair:]
+        if k < STEPS - 1:
+            span = range(n % 2 * pair // 2, (n % 2 + 1) * pair // 2)
+        else:
+            span = range(pair)
+        for c in span:
+            lag(c, k)
+
+    acts = {"s": spread, "f": forward, "t": relay, "c": finish, "b": prepare, "m": combine, "e": emit, "g": early, "p": place}
     for act, n in ORDER:
         acts[act](n)
 
@@ -300,6 +316,7 @@
             pltpu.VMEM((channels // 2, 2 * block), jnp.float32),
             pltpu.VMEM((channels, LANES), jnp.float32),
             pltpu.VMEM(((LAGS + 1) * channels, block), jnp.float32),
+            pltpu.VMEM((channels // 2, LAGS, 2 * block), jnp.float32),
             pltpu.SemaphoreType.DMA((STEPS, PIECES, grps)),
             pltpu.SemaphoreType.DMA((STEPS - 1, PIECES, 2)),
             pltpu.SemaphoreType.DMA((STEPS, PIECES, 3)),

time: 40.2 us -> 38.9 us (0.968)
  Pallas kernels: 38.2 us -> 37.1 us
    pallas_call x1, Pallas kernels: 38.2 us -> 37.1 us  [on_device(): pl.pallas_call(functools.partial(kernel, blks, grps, (channels, segs, bin...]
where the time goes in v4:
time: 38.9 us; the launch traced here: 38.8 us
  Pallas kernels  37.1 us (95%)
  local copies, waits for them, and re-layouts  1.67 us (4%)
    pallas_call x1, Pallas kernels, on_device(): pl.pallas_call(functools.partial(kernel, blks, grps, (channels, segs, bin...  37.1 us
    unnamed x1, local copies, waits for them, and re-layouts  1.67 us

profile of v4, /device:TPU:0, one launch (start us, length us, event | category | flops | bytes accessed | tf_op | source)
XLA Modules:
  0.0 38.8 jit_solution(11232608397672511794)
XLA Ops:
  0.0 37.1 %shard_map.55 = (bf16[256,3,16,128]{3,2,1,0:T(8,128)(2,1)S(1)}, f32[16,384]{1,0:T(8,128)}) custom-call(bf16[128,1024]{1,0:T(8,128)(2,1)} %bitcast.4, s32[8,16]{1,0:T(8,128)} %bitcast.5, bf16[128,128]{1,0:T(8,128)(2,1)} %constant.8.clone.row_ref, bf16[1024,1024]{1,0:T(8,128)(2,1)} %constant.11.hi_hbm, bf16[256,1024]{1,0:T(8,128)(2,1)} %constant.12.lag_hbm), custom_call_target="tpu_custom_call" | custom-call | tf_op jit(solution)/shard_map/pallas_call | solution.py:300
  37.1 1.7 %copy.7 = bf16[256,16,3,128]{3,1,2,0:T(8,128)(2,1)} copy(bf16[256,16,3,128]{3,1,2,0:T(8,128)(2,1)S(1)} %bitcast.3) | data formatting | bytes 6291456

commit v5 on v4

--- a/solution.py
+++ b/solution.py
@@ -13,6 +13,7 @@
 STEPS = 3
 LANES = 128
 GROUP = 16
+TURNS = 4
 SPLIT = (0, 1, 2)
 PIECES = len(SPLIT) - 1
 CLIMB = ((1, 0), (1, 1), (2, 1))
@@ -37,15 +38,6 @@
     return both.astype(ml_dtypes.bfloat16)
 
 
-def row_table(channels, segs):
-    table = np.zeros((segs, channels, channels, segs), np.float32)
-    for s in range(segs):
-        for c in range(channels):
-            table[s, c, c, s] = 1.0
-    size = segs * channels
-    return table.reshape(size, size).astype(ml_dtypes.bfloat16)
-
-
 def mm(a, b):
     return jnp.dot(a, b, preferred_element_type=jnp.float32)
 
@@ -56,18 +48,21 @@
 
 def kernel(
     blks, grps, dims, normalise,
-    rec_ref, flag_ref, row_ref, hi_hbm, lag_hbm,
+    rec_hbm, flag_hbm, hi_hbm, lag_hbm,
     out_ref, count_ref,
-    hi_ref, perm_ref, lag_ref, load_sem, buf, diag, cross, inv, wide, stage, acc, recv_sem, hop_sem, peer_sem, sib_sem,
+    rec_ref, flag_ref, hi_ref, perm_ref, lag_ref, load_sem, buf, diag, cross, inv, wide, stage, acc, recv_sem, hop_sem, peer_sem, sib_sem,
 ):
     channels, segs, bins, half = dims
     width = half * 2 * segs
     chunks = half // GROUP
     pair = channels // 2
+    depth = hi_hbm.shape[0] // TURNS
+    parts = [pl.ds(n * depth, depth) for n in range(TURNS)]
     loads = [
         pltpu.make_async_copy(source, target, load_sem.at[n])
         for n, (source, target) in enumerate(
-            ((hi_hbm, hi_ref), (lag_hbm, lag_ref)))
+            [(rec_hbm, rec_ref), (flag_hbm, flag_ref)]
+            + [(hi_hbm.at[rows], hi_ref.at[rows]) for rows in parts] + [(lag_hbm, lag_ref)])
     ]
     for load in loads[:-1]:
         load.start()
@@ -93,9 +88,16 @@
     lane = lax.broadcasted_iota(jnp.int32, (segs * LANES, LANES), 1)
     for q in range(per):
         perm_ref[:, q * LANES:(q + 1) * LANES] = jnp.where(goes == lane + q * LANES, 1.0, 0.0).astype(jnp.bfloat16)
-    rec = mm(row_ref[...], rec_ref[...]).astype(jnp.bfloat16)
+    came = lax.broadcasted_iota(jnp.int32, (segs * channels, segs * channels), 0)
+    goes = came % channels * segs + came // channels
+    order = jnp.where(goes == lax.broadcasted_iota(jnp.int32, came.shape, 1), 1.0, 0.0).astype(jnp.bfloat16)
     loads[0].wait()
-    spec = mm(rec, hi_ref[...])
+    rec = mm(order, rec_ref[...]).astype(jnp.bfloat16)
+    spec = 0.0
+    for n in range(TURNS):
+        loads[2 + n].wait()
+        spec = spec + mm(rec[:, n * depth:(n + 1) * depth], hi_ref[parts[n]])
+    loads[1].wait()
     real = spec[:, :bins]
     imag = spec[:, bins:]
     power = real * real + imag * imag
@@ -301,15 +303,17 @@
         functools.partial(kernel, blks, grps, (channels, segs, bins, half), splits == 1),
         out_shape=(
             pltpu.VMEM((LAGS, STEPS, channels, block), jnp.bfloat16),
-            jax.ShapeDtypeStruct((channels, STEPS * block), jnp.float32),
+            pltpu.VMEM((channels, STEPS * block), jnp.float32),
         ),
-        in_specs=[vmem] * 3 + [pl.BlockSpec(memory_space=pltpu.HBM)] * 2,
+        in_specs=[pl.BlockSpec(memory_space=pltpu.HBM)] * 4,
         out_specs=(vmem, vmem),
         scratch_shapes=[
+            pltpu.VMEM((channels * segs, length), jnp.bfloat16),
+            pltpu.VMEM((segs, channels), jnp.int32),
             pltpu.VMEM((length, 2 * bins), jnp.bfloat16),
             pltpu.VMEM((segs * LANES, segs * LANES), jnp.bfloat16),
             pltpu.VMEM((LAGS, 2 * half), jnp.bfloat16),
-            pltpu.SemaphoreType.DMA((2,)),
+            pltpu.SemaphoreType.DMA((3 + TURNS,)),
             pltpu.VMEM((STEPS, grps, channels, width), jnp.bfloat16),
             pltpu.VMEM((half // GROUP, channels * GROUP, 2 * segs * GROUP), jnp.bfloat16),
             pltpu.VMEM((channels // 2, 2, half, 2 * block), jnp.bfloat16),
@@ -328,7 +332,6 @@
     )(
         records.reshape(channels * segs, length),
         flags.T,
-        jnp.asarray(row_table(channels, segs)),
         high.reshape(length, 2 * bins),
         lags.reshape(LAGS, 2 * half),
     )

time: 38.9 us -> 37.8 us (0.972)
  Pallas kernels: 37.1 us -> 36 us
    pallas_call x1, Pallas kernels: 37.1 us -> 36 us  [on_device(): pl.pallas_call(functools.partial(kernel, blks, grps, (channels, segs, bin...]
where the time goes in v5:
time: 37.8 us; the launch traced here: 37.7 us
  Pallas kernels  36 us (95%)
  local copies, waits for them, and re-layouts  1.67 us (4%)
    pallas_call x1, Pallas kernels, on_device(): pl.pallas_call(functools.partial(kernel, blks, grps, (channels, segs, bin...  36 us
    unnamed x1, local copies, waits for them, and re-layouts  1.67 us

profile of v5, /device:TPU:0, one launch (start us, length us, event | category | flops | bytes accessed | tf_op | source)
XLA Modules:
  0.0 37.7 jit_solution(1508712735034940717)
XLA Ops:
  0.0 36.0 %shard_map.46 = (bf16[256,3,16,128]{3,2,1,0:T(8,128)(2,1)S(1)}, f32[16,384]{1,0:T(8,128)}) custom-call(bf16[128,1024]{1,0:T(8,128)(2,1)} %bitcast.4, s32[8,16]{1,0:T(8,128)} %bitcast.5, bf16[1024,1024]{1,0:T(8,128)(2,1)} %constant.8.hi_hbm, bf16[256,1024]{1,0:T(8,128)(2,1)} %constant.9.lag_hbm), custom_call_target="tpu_custom_call" | custom-call | tf_op jit(solution)/shard_map/pallas_call | solution.py:302
  36.0 1.7 %copy.6 = bf16[256,16,3,128]{3,1,2,0:T(8,128)(2,1)} copy(bf16[256,16,3,128]{3,1,2,0:T(8,128)(2,1)S(1)} %bitcast.3) | data formatting | bytes 6291456

commit v6 on v5

--- a/solution.py
+++ b/solution.py
@@ -15,10 +15,11 @@
 GROUP = 16
 TURNS = 4
 SPLIT = (0, 1, 2)
+LAST = 4
 PIECES = len(SPLIT) - 1
 CLIMB = ((1, 0), (1, 1), (2, 1))
 ORDER = (
-    ("s", 0), ("s", 1), ("f", 0), ("t", 0), ("b", 0), ("s", 2), ("f", 1), ("s", 3), ("c", 0), ("m", 0), ("s", 4), ("t", 1), ("f", 2), ("c", 1), ("t", 2), ("s", 5), ("b", 1), ("c", 2), ("m", 1), ("t", 3), ("f", 3), ("e", 0), ("e", 1), ("p", 0), ("c", 3), ("f", 4), ("m", 2), ("t", 4), ("t", 5), ("f", 5), ("m", 3), ("c", 4), ("e", 2), ("e", 3), ("p", 1), ("c", 5), ("m", 4), ("g", 0), ("g", 1), ("m", 5), ("e", 4), ("p", 2),
+    ("s", 0), ("s", 1), ("f", 0), ("t", 0), ("b", 0), ("s", 2), ("f", 1), ("s", 3), ("c", 0), ("m", 0), ("s", 4), ("t", 1), ("f", 2), ("c", 1), ("t", 2), ("s", 5), ("b", 1), ("c", 2), ("m", 1), ("t", 3), ("f", 3), ("e", 0), ("e", 1), ("p", 0), ("c", 3), ("f", 4), ("m", 2), ("t", 4), ("t", 5), ("f", 5), ("m", 3), ("c", 4), ("e", 2), ("e", 3), ("p", 1), ("c", 5), ("m", 4), ("g", 0), ("g", 1), ("m", 5), ("e", 4),
 )
 MESH = pl.DeviceIdType.MESH
 
@@ -38,6 +39,14 @@
     return both.astype(ml_dtypes.bfloat16)
 
 
+def early_bins(half):
+    return half // GROUP * SPLIT[-2] // SPLIT[-1] * GROUP // LANES * LANES
+
+
+def columns(ref, half, low, high):
+    return jnp.concatenate([ref[:, i * half + low:i * half + high] for i in range(2)], axis=1)
+
+
 def mm(a, b):
     return jnp.dot(a, b, preferred_element_type=jnp.float32)
 
@@ -49,8 +58,8 @@
 def kernel(
     blks, grps, dims, normalise,
     rec_hbm, flag_hbm, hi_hbm, lag_hbm,
-    out_ref, count_ref,
-    rec_ref, flag_ref, hi_ref, perm_ref, lag_ref, load_sem, buf, diag, cross, inv, wide, stage, acc, recv_sem, hop_sem, peer_sem, sib_sem,
+    out_ref, cross, acc, inv, lag_ref, count_ref,
+    rec_ref, flag_ref, hi_ref, perm_ref, load_sem, buf, diag, wide, stage, recv_sem, hop_sem, peer_sem, sib_sem,
 ):
     channels, segs, bins, half = dims
     width = half * 2 * segs
@@ -220,21 +229,15 @@
             for p in range(2):
                 cross[:, i, q * GROUP:(q + 1) * GROUP, p * block:(p + 1) * block] = product[i, p]
 
-    begun = bounds[-2] * GROUP // LANES * LANES
-
-    def table(low, high):
-        return jnp.concatenate([lag_ref[:, i * half + low:i * half + high] for i in range(2)], axis=1)
+    begun = early_bins(half)
 
     def early(j):
         if begun:
             for c in range(j * pair // 2, (j + 1) * pair // 2):
-                acc[c] = mm(table(0, begun), cross[c, :, :begun].reshape(2 * begun, 2 * block))
-
-    def lag(c, k):
-        if begun and k == STEPS - 1:
-            total = acc[c] + mm(table(begun, half), cross[c, :, begun:].reshape(2 * (half - begun), 2 * block))
-        else:
-            total = mm(lag_ref[...], cross[c].reshape(2 * half, 2 * block))
+                acc[c] = mm(columns(lag_ref, half, 0, begun), cross[c, :, :begun].reshape(2 * begun, 2 * block))
+
+    def lag(c):
+        total = mm(lag_ref[...], cross[c].reshape(2 * half, 2 * block))
         if normalise:
             total = total * inv[c:c + 1, :]
         stage[pl.ds(c, LAGS, stride=channels), :] = total[:, :block]
@@ -266,11 +269,8 @@
             inv[:, :block] = factor[:pair]
             inv[:, block:] = factor[pair:]
         if k < STEPS - 1:
-            span = range(n % 2 * pair // 2, (n % 2 + 1) * pair // 2)
-        else:
-            span = range(pair)
-        for c in span:
-            lag(c, k)
+            for c in range(n % 2 * pair // 2, (n % 2 + 1) * pair // 2):
+                lag(c)
 
     acts = {"s": spread, "f": forward, "t": relay, "c": finish, "b": prepare, "m": combine, "e": emit, "g": early, "p": place}
     for act, n in ORDER:
@@ -278,6 +278,33 @@
 
     for copy in sent:
         copy.wait_send()
+
+
+def last_kernel(normalise, first_ref, cross, acc, inv, lag_ref, out_hbm, stage, tail, sems):
+    pair, half = cross.shape[0], cross.shape[2]
+    channels, block = 2 * pair, cross.shape[3] // 2
+    begun = early_bins(half)
+    first = pltpu.make_async_copy(first_ref, out_hbm.at[:, pl.ds(0, STEPS - 1)], sems.at[LAST])
+    first.start()
+    for c in range(pair):
+        total = mm(columns(lag_ref, half, begun, half), cross[c, :, begun:].reshape(2 * (half - begun), 2 * block))
+        if begun:
+            total = acc[c] + total
+        if normalise:
+            total = total * inv[c:c + 1, :]
+        stage[pl.ds(c, LAGS, stride=channels), :] = total[:, :block]
+        stage[pl.ds(c + pair, LAGS, stride=channels), :] = total[:, block:]
+    span = LAGS // LAST
+    copies = []
+    for m in range(LAST):
+        for n in range(m * span // 16, (m + 1) * span // 16):
+            part = stage[n * 16 * channels:(n + 1) * 16 * channels, :]
+            tail[n * 16:(n + 1) * 16] = part.astype(jnp.bfloat16).reshape(16, channels, block)
+        rows = pl.ds(m * span, span)
+        copies.append(pltpu.make_async_copy(tail.at[rows], out_hbm.at[rows, STEPS - 1], sems.at[m]))
+        copies[-1].start()
+    for copy in copies + [first]:
+        copy.wait()
 
 
 def on_device(records, flags):
@@ -299,35 +326,35 @@
         lags = lax.dynamic_slice_in_dim(lags, first, half, 2)
     width = half * 2 * segs + LANES
     vmem = pl.BlockSpec(memory_space=pltpu.VMEM)
-    out, count = pl.pallas_call(
+    first, cross, acc, inv, lags, count = pl.pallas_call(
         functools.partial(kernel, blks, grps, (channels, segs, bins, half), splits == 1),
         out_shape=(
-            pltpu.VMEM((LAGS, STEPS, channels, block), jnp.bfloat16),
+            pltpu.VMEM((LAGS, STEPS - 1, channels, block), jnp.bfloat16),
+            pltpu.VMEM((channels // 2, 2, half, 2 * block), jnp.bfloat16),
+            pltpu.VMEM((channels // 2, LAGS, 2 * block), jnp.float32),
+            pltpu.VMEM((channels // 2, 2 * block), jnp.float32),
+            pltpu.VMEM((LAGS, 2 * half), jnp.bfloat16),
             pltpu.VMEM((channels, STEPS * block), jnp.float32),
         ),
         in_specs=[pl.BlockSpec(memory_space=pltpu.HBM)] * 4,
-        out_specs=(vmem, vmem),
+        out_specs=(vmem,) * 6,
         scratch_shapes=[
             pltpu.VMEM((channels * segs, length), jnp.bfloat16),
             pltpu.VMEM((segs, channels), jnp.int32),
             pltpu.VMEM((length, 2 * bins), jnp.bfloat16),
             pltpu.VMEM((segs * LANES, segs * LANES), jnp.bfloat16),
-            pltpu.VMEM((LAGS, 2 * half), jnp.bfloat16),
             pltpu.SemaphoreType.DMA((3 + TURNS,)),
             pltpu.VMEM((STEPS, grps, channels, width), jnp.bfloat16),
             pltpu.VMEM((half // GROUP, channels * GROUP, 2 * segs * GROUP), jnp.bfloat16),
-            pltpu.VMEM((channels // 2, 2, half, 2 * block), jnp.bfloat16),
-            pltpu.VMEM((channels // 2, 2 * block), jnp.float32),
             pltpu.VMEM((channels, LANES), jnp.float32),
             pltpu.VMEM(((LAGS + 1) * channels, block), jnp.float32),
-            pltpu.VMEM((channels // 2, LAGS, 2 * block), jnp.float32),
             pltpu.SemaphoreType.DMA((STEPS, PIECES, grps)),
             pltpu.SemaphoreType.DMA((STEPS - 1, PIECES, 2)),
             pltpu.SemaphoreType.DMA((STEPS, PIECES, 3)),
             pltpu.SemaphoreType.DMA((STEPS, PIECES, grps // 2)),
         ],
         compiler_params=pltpu.CompilerParams(
-            collective_id=0, has_side_effects=True, vmem_limit_bytes=52 * 1024 * 1024
+            collective_id=0, has_side_effects=True, vmem_limit_bytes=54 * 1024 * 1024
         ),
     )(
         records.reshape(channels * segs, length),
@@ -335,6 +362,18 @@
         high.reshape(length, 2 * bins),
         lags.reshape(LAGS, 2 * half),
     )
+    out = pl.pallas_call(
+        functools.partial(last_kernel, splits == 1),
+        out_shape=jax.ShapeDtypeStruct((LAGS, STEPS, channels, block), jnp.bfloat16),
+        in_specs=[vmem] * 5,
+        out_specs=pl.BlockSpec(memory_space=pltpu.HBM),
+        scratch_shapes=[
+            pltpu.VMEM(((LAGS + 1) * channels, block), jnp.float32),
+            pltpu.VMEM((LAGS, channels, block), jnp.bfloat16),
+            pltpu.SemaphoreType.DMA((LAST + 1,)),
+        ],
+        compiler_params=pltpu.CompilerParams(vmem_limit_bytes=32 * 1024 * 1024),
+    )(first, cross, acc, inv, lags)
     out = out.transpose(0, 2, 1, 3)
     if splits > 1:
         out = lax.psum_scatter(out, "sub", scatter_dimension=0, tiled=True).astype(jnp.float32)

time: 37.8 us -> 37.2 us (0.984)
  local copies, waits for them, and re-layouts: 1.67 us -> 0 us
  Pallas kernels: 36 us -> 37 us
    pallas_call x0 -> x1, Pallas kernels: none -> 2.01 us  [on_device(): pl.pallas_call(functools.partial(last_kernel, splits == 1), out_shape=jax...]
    unnamed x1 -> x0, local copies, waits for them, and re-layouts: 1.67 us -> none
    pallas_call x1, Pallas kernels: 36 us -> 35 us  [on_device(): pl.pallas_call(functools.partial(kernel, blks, grps, (channels, segs, bin...]
where the time goes in v6:
time: 37.2 us; the launch traced here: 37 us
  Pallas kernels  37 us (99%)
    pallas_call x1, Pallas kernels, on_device(): pl.pallas_call(functools.partial(kernel, blks, grps, (channels, segs, bin...  35 us
    pallas_call x1, Pallas kernels, on_device(): pl.pallas_call(functools.partial(last_kernel, splits == 1), out_shape=jax...  2.01 us

profile of v6, /device:TPU:0, one launch (start us, length us, event | category | flops | bytes accessed | tf_op | source)
XLA Modules:
  0.0 37.0 jit_solution(1725531622912049466)
XLA Ops:
  0.0 35.0 %shard_map.46 = (bf16[256,2,16,128]{3,2,1,0:T(8,128)(2,1)S(1)}, bf16[8,2,512,256]{3,2,1,0:T(8,128)(2,1)S(1)}, f32[8,256,256]{2,1,0:T(8,128)S(1)}, f32[8,256]{1,0...) custom-call(bf16[128,1024]{1,0:T(8,128)(2,1)} %bitcast.3, s32[8,16]{1,0:T(8,128)} %bitcast.4, ...), custom_call_target="tpu_custom_call" | custom-call | tf_op jit(solution)/shard_map/pallas_call | solution.py:329
  35.0 2.0 %shard_map.47 = bf16[256,3,16,128]{3,2,1,0:T(8,128)(2,1)} custom-call(bf16[256,2,16,128]{3,2,1,0:T(8,128)(2,1)S(1)} %get-tuple-element.10.first_ref, bf16[8,2,512,256]{3,2,1,0:T(8,128)(2,1)S(1)} %get-tuple-element.11.cross, f32[8,256,256]{2,1,0:T(8,128)S(1)} %get-tuple-element.12.acc, f32[8,256]{1,0:T(8,128)S(1)} %get-tuple-element.13.inv, ...), custom_call_target="tpu_custom_call" | custom-call | tf_op jit(solution)/shard_map/pallas_call | solution.py:365

commit v7 on v6

--- a/solution.py
+++ b/solution.py
@@ -17,7 +17,7 @@
 SPLIT = (0, 1, 2)
 LAST = 4
 PIECES = len(SPLIT) - 1
-CLIMB = ((1, 0), (1, 1), (2, 1))
+CLIMB = ((1, 0), (1, 1), (2, 0))
 ORDER = (
     ("s", 0), ("s", 1), ("f", 0), ("t", 0), ("b", 0), ("s", 2), ("f", 1), ("s", 3), ("c", 0), ("m", 0), ("s", 4), ("t", 1), ("f", 2), ("c", 1), ("t", 2), ("s", 5), ("b", 1), ("c", 2), ("m", 1), ("t", 3), ("f", 3), ("e", 0), ("e", 1), ("p", 0), ("c", 3), ("f", 4), ("m", 2), ("t", 4), ("t", 5), ("f", 5), ("m", 3), ("c", 4), ("e", 2), ("e", 3), ("p", 1), ("c", 5), ("m", 4), ("g", 0), ("g", 1), ("m", 5), ("e", 4),
 )

time: 37.2 us -> 36.7 us (0.987)
  Pallas kernels: 37 us -> 36.5 us
    pallas_call x1, Pallas kernels: 35 us -> 34.5 us  [on_device(): pl.pallas_call(functools.partial(kernel, blks, grps, (channels, segs, bin...]
where the time goes in v7:
time: 36.7 us; the launch traced here: 36.6 us
  Pallas kernels  36.5 us (99%)
    pallas_call x1, Pallas kernels, on_device(): pl.pallas_call(functools.partial(kernel, blks, grps, (channels, segs, bin...  34.5 us
    pallas_call x1, Pallas kernels, on_device(): pl.pallas_call(functools.partial(last_kernel, splits == 1), out_shape=jax...  2.01 us

profile of v7, /device:TPU:0, one launch (start us, length us, event | category | flops | bytes accessed | tf_op | source)
XLA Modules:
  0.0 36.6 jit_solution(17695333843117735760)
XLA Ops:
  0.0 34.5 %shard_map.46 = (bf16[256,2,16,128]{3,2,1,0:T(8,128)(2,1)S(1)}, bf16[8,2,512,256]{3,2,1,0:T(8,128)(2,1)S(1)}, f32[8,256,256]{2,1,0:T(8,128)S(1)}, f32[8,256]{1,0...) custom-call(bf16[128,1024]{1,0:T(8,128)(2,1)} %bitcast.3, s32[8,16]{1,0:T(8,128)} %bitcast.4, ...), custom_call_target="tpu_custom_call" | custom-call | tf_op jit(solution)/shard_map/pallas_call | solution.py:329
  34.5 2.0 %shard_map.47 = bf16[256,3,16,128]{3,2,1,0:T(8,128)(2,1)} custom-call(bf16[256,2,16,128]{3,2,1,0:T(8,128)(2,1)S(1)} %get-tuple-element.10.first_ref, bf16[8,2,512,256]{3,2,1,0:T(8,128)(2,1)S(1)} %get-tuple-element.11.cross, f32[8,256,256]{2,1,0:T(8,128)S(1)} %get-tuple-element.12.acc, f32[8,256]{1,0:T(8,128)S(1)} %get-tuple-element.13.inv, ...), custom_call_target="tpu_custom_call" | custom-call | tf_op jit(solution)/shard_map/pallas_call | solution.py:365

commit v8 on v7

--- a/solution.py
+++ b/solution.py
@@ -172,10 +172,10 @@
         k, h = steps[n]
         if k:
             arrived(k, h, g)
+        give(k, h, g, 0, target, peer_sem)
+        give(k, h, g, 1, source, peer_sem)
         if k + 1 < STEPS:
             rise(k, h, g, 0)
-        give(k, h, g, 0, target, peer_sem)
-        give(k, h, g, 1, source, peer_sem)
         give(k, h, g, 0, sib, sib_sem)
 
     def forward(n):

time: 36.7 us -> 36.7 us (level)
  no operation moved by 1% of the time
where the time goes in v8:
time: 36.7 us; the launch traced here: 36.6 us
  Pallas kernels  36.5 us (99%)
    pallas_call x1, Pallas kernels, on_device(): pl.pallas_call(functools.partial(kernel, blks, grps, (channels, segs, bin...  34.5 us
    pallas_call x1, Pallas kernels, on_device(): pl.pallas_call(functools.partial(last_kernel, splits == 1), out_shape=jax...  2.01 us

profile of v8, /device:TPU:0, one launch (start us, length us, event | category | flops | bytes accessed | tf_op | source)
XLA Modules:
  0.0 36.6 jit_solution(642384807757514149)
XLA Ops:
  0.0 34.5 %shard_map.46 = (bf16[256,2,16,128]{3,2,1,0:T(8,128)(2,1)S(1)}, bf16[8,2,512,256]{3,2,1,0:T(8,128)(2,1)S(1)}, f32[8,256,256]{2,1,0:T(8,128)S(1)}, f32[8,256]{1,0...) custom-call(bf16[128,1024]{1,0:T(8,128)(2,1)} %bitcast.3, s32[8,16]{1,0:T(8,128)} %bitcast.4, ...), custom_call_target="tpu_custom_call" | custom-call | tf_op jit(solution)/shard_map/pallas_call | solution.py:329
  34.5 2.0 %shard_map.47 = bf16[256,3,16,128]{3,2,1,0:T(8,128)(2,1)} custom-call(bf16[256,2,16,128]{3,2,1,0:T(8,128)(2,1)S(1)} %get-tuple-element.10.first_ref, bf16[8,2,512,256]{3,2,1,0:T(8,128)(2,1)S(1)} %get-tuple-element.11.cross, f32[8,256,256]{2,1,0:T(8,128)S(1)} %get-tuple-element.12.acc, f32[8,256]{1,0:T(8,128)S(1)} %get-tuple-element.13.inv, ...), custom_call_target="tpu_custom_call" | custom-call | tf_op jit(solution)/shard_map/pallas_call | solution.py:365
